TPU v7x, 32 devices: a whole 2x2x4 slice. The times are simulated.
32 devices in a mesh: groups: 2 (over y), gy: 16 (over z, x, core), gx: 1.
Axes of the slice: x: 2, y: 2, z: 4, core: 2. Of those that a mesh axis runs over, the one named last changes fastest.
Arguments:
- state: bfloat16 [6, 64, 512, 128], P('groups', None, 'gy', 'gx'), parts along dimension 0, may hold values from -6 to 6
- obs_value: float32 [2048], P(('groups', 'gy', 'gx')), parts along dimension 0, may hold values from -6 to 6
- obs_sigma: float32 [2048], P(('groups', 'gy', 'gx')), parts along dimension 0, may hold values from 0.5 to 2
- obs_pixel: int32 [2048], P(('groups', 'gy', 'gx')), parts along dimension 0, may hold values from 0 to 4095
- obs_route: int32 [2048, 1], P(('groups', 'gy', 'gx')), parts along dimension 0, may hold values from 0 to 15; in each aligned block of 64 rows (0 to 63, 64 to 127, ...) at most 8 rows name the same one
- obs_count: int32 [32], P(('groups', 'gy', 'gx')), parts along dimension 0, may hold values from 32 to 64
- radius: int32 [32, 4], P('groups'), parts along dimension 0, may hold values from 17 to 32
Outputs:
- analysis: bfloat16 [6, 64, 512, 128], P('groups', None, 'gy', 'gx'), parts along dimension 0
There are 2 independent parts, one for each index of `groups`. A program takes and returns all parts, laid end to end along the dimension named above; each array names one. Nothing has to cross between parts.
Inputs may be any that keep to these rules, and one draw needn't show every extreme that they name: `obs_route`: among the 64 slots that arrive at one device, no tile row is named more than 8 times, and in some devices' slots one tile row is named exactly 8 times.
All inputs are finite; a program needn't handle non-finite values.
Results may differ from a plain program's by a relative error of at most 0.0057.
Values may be sent and summed in bfloat16 or wider, within the bound.
A program may use at most 64 MiB of HBM per device.

v0:
```python
import jax
import jax.numpy as jnp
import numpy as np
from jax import lax
from jax.sharding import PartitionSpec as P

STRIDE = 32
ITER_NS = 6
OBS_PEER = 4


def with_halo(cells, sides, width):
    for axis, dim in sides:
        count = lax.axis_size(axis)
        ends = count - 1
        head = lax.slice_in_dim(cells, 0, width, axis=dim)
        tail = lax.slice_in_dim(cells, cells.shape[dim] - width, cells.shape[dim], axis=dim)
        cells = jnp.concatenate(
            [
                lax.ppermute(tail, axis, [(i, (i + 1) % count) for i in range(ends)]),
                cells,
                lax.ppermute(head, axis, [((i + 1) % count, i) for i in range(ends)]),
            ],
            axis=dim,
        )
    return cells


def obs_operator(values):
    return values[1] * jax.nn.sigmoid(values[0]) - 0.5 * values[2]


def taper_weight(row_offset, col_offset, own_radius):
    distance = row_offset * row_offset + col_offset * col_offset
    squared = own_radius * own_radius
    fraction = distance / squared
    return jnp.where(distance < squared, (1.0 - fraction) * (1.0 - fraction), 0.0)


def solve_weights(gram_matrix, members):
    spread = gram_matrix[..., :members, :]
    forcing = gram_matrix[..., members, :]
    identity = jnp.eye(members, dtype=jnp.float32)
    matrix = identity + spread / (members - 1.0)
    norm_scale = jnp.sqrt(jnp.sum(matrix * matrix, axis=(-2, -1), keepdims=True))
    current = matrix / norm_scale
    inverse_root = jnp.broadcast_to(identity, matrix.shape)
    for iteration in range(ITER_NS):
        factor = 1.5 * identity - 0.5 * jnp.matmul(
            inverse_root, current, precision=lax.Precision.HIGHEST
        )
        current = jnp.matmul(current, factor, precision=lax.Precision.HIGHEST)
        inverse_root = jnp.matmul(factor, inverse_root, precision=lax.Precision.HIGHEST)
    square_root = inverse_root / jnp.sqrt(norm_scale)
    pulled = jnp.einsum("...ij,...j->...i", square_root, forcing, precision=lax.Precision.HIGHEST)
    mean_shift = jnp.einsum(
        "...ij,...j->...i", square_root, pulled, precision=lax.Precision.HIGHEST
    ) / (members - 1.0)
    return (square_root + mean_shift[..., :, None]).astype(jnp.bfloat16)


def body(state, obs_value, obs_sigma, obs_pixel, obs_route, obs_count, radius):
    fields, members, tile_rows, tile_cols = state.shape
    row_devices = lax.axis_size("gy")
    col_devices = lax.axis_size("gx")
    row_index = lax.axis_index("gy")
    col_index = lax.axis_index("gx")
    stride = STRIDE
    half_step = stride // 2
    point_rows = tile_rows // stride
    point_cols = tile_cols // stride
    arrivals = obs_value.shape[0]
    capacity = 2 * OBS_PEER
    slot_count = capacity * row_devices
    present = jnp.arange(arrivals) < obs_count[0]
    inverse_sigma = jnp.where(present, 1.0 / obs_sigma, 0.0)
    target_row = obs_route[:, 0]
    one_hot = (target_row[:, None] == jnp.arange(row_devices)[None, :]).astype(jnp.int32)
    slot_rank = jnp.sum((jnp.cumsum(one_hot, axis=0) - one_hot) * one_hot, axis=1)
    placement = target_row * capacity + slot_rank
    record = jnp.stack([obs_value, inverse_sigma, obs_pixel.astype(jnp.float32)])
    outgoing = jnp.zeros((3, slot_count), jnp.float32).at[:, placement].set(record)
    incoming = lax.all_to_all(outgoing, "gy", split_axis=1, concat_axis=1, tiled=True)
    pixels = incoming[2].astype(jnp.int32)
    flattened = state.reshape(fields, members, tile_rows * tile_cols)
    picked = jnp.take(flattened, pixels, axis=2).astype(jnp.float32)
    predicted = obs_operator(picked)
    centre = jnp.mean(predicted, axis=0)
    spread_rows = (predicted - centre) * incoming[1]
    misfit = (incoming[0] - centre) * incoming[1]
    obs_row = (pixels // tile_cols).astype(jnp.float32)
    obs_col = (pixels % tile_cols).astype(jnp.float32)
    packed = jnp.concatenate(
        [spread_rows, misfit[None], obs_row[None], obs_col[None]], axis=0
    ).astype(jnp.bfloat16)
    own_radius = lax.dynamic_slice(
        radius, (row_index * point_rows, col_index * point_cols), (point_rows, point_cols)
    ).astype(jnp.float32)
    beside_all = with_halo(packed[None, None], (("gy", 0), ("gx", 1)), 1)
    weighted_rows = beside_all[:, :, : members + 1, :]
    spreads = beside_all[:, :, :members, :]
    near_rows = (
        beside_all[:, :, members + 1, :].astype(jnp.float32)
        + ((jnp.arange(3) - 1) * tile_rows).astype(jnp.float32)[:, None, None]
    )
    near_cols = (
        beside_all[:, :, members + 2, :].astype(jnp.float32)
        + ((jnp.arange(3) - 1) * tile_cols).astype(jnp.float32)[None, :, None]
    )
    gram_list = []
    for point_col in range(point_cols):
        nearness = taper_weight(
            near_rows - half_step,
            near_cols - (stride * point_col + half_step),
            own_radius[0, point_col],
        )
        scaled = (nearness[:, :, None, :] * weighted_rows).astype(jnp.bfloat16)
        gram_list.append(
            jnp.einsum("abis,abjs->ij", scaled, spreads, preferred_element_type=jnp.float32)
        )
    gram_sum = jnp.stack(gram_list).reshape(point_rows, point_cols, members + 1, members)
    weights = solve_weights(gram_sum, members)
    framed = with_halo(
        weights.reshape(point_rows, point_cols, members * members), (("gy", 0), ("gx", 1)), 1
    )
    framed = framed.at[0].set(jnp.where(row_index == 0, framed[1], framed[0]))
    framed = framed.at[point_rows + 1].set(
        jnp.where(row_index == row_devices - 1, framed[point_rows], framed[point_rows + 1])
    )
    framed = framed.at[:, 0].set(jnp.where(col_index == 0, framed[:, 1], framed[:, 0]))
    framed = framed.at[:, point_cols + 1].set(
        jnp.where(col_index == col_devices - 1, framed[:, point_cols], framed[:, point_cols + 1])
    )
    framed = framed.reshape(point_rows + 2, point_cols + 2, members, members)
    centre_state = jnp.mean(state, axis=1, dtype=jnp.float32)
    anomaly = (state.astype(jnp.float32) - centre_state[:, None]).astype(jnp.bfloat16)
    pieces = anomaly.reshape(fields, members, 2 * point_rows, half_step, 2 * point_cols, half_step)
    upper_index = (np.arange(2 * point_rows) + 1) // 2
    left_index = (np.arange(2 * point_cols) + 1) // 2
    row_fraction = jnp.asarray(
        ((np.arange(tile_rows) + half_step) % stride / stride)
        .astype(np.float32)
        .reshape(2 * point_rows, half_step)
    )
    col_fraction = jnp.asarray(
        ((np.arange(tile_cols) + half_step) % stride / stride)
        .astype(np.float32)
        .reshape(2 * point_cols, half_step)
    )
    analysis = centre_state.reshape(fields, 1, 2 * point_rows, half_step, 2 * point_cols, half_step)
    for down_step in (0, 1):
        for right_step in (0, 1):
            corner = framed[upper_index + down_step][:, left_index + right_step]
            product = jnp.einsum(
                "fkhasb,hskm->fmhasb", pieces, corner, preferred_element_type=jnp.float32
            )
            row_weight = row_fraction if down_step else 1.0 - row_fraction
            col_weight = col_fraction if right_step else 1.0 - col_fraction
            blend = row_weight[:, :, None, None] * col_weight[None, None]
            analysis = analysis + blend * product
    return analysis.reshape(fields, members, tile_rows, tile_cols).astype(jnp.bfloat16)


def solution(mesh):
    placed = (
        P("groups", None, "gy", "gx"),
        P(("groups", "gy", "gx")),
        P(("groups", "gy", "gx")),
        P(("groups", "gy", "gx")),
        P(("groups", "gy", "gx"), None),
        P(("groups", "gy", "gx")),
        P("groups", None),
    )
    return jax.shard_map(
        body, mesh=mesh, in_specs=placed, out_specs=P("groups", None, "gy", "gx"), check_vma=False
    )
```

profile of v0, /device:TPU:3, one launch (start us, length us, event | category | flops | bytes accessed | tf_op | source)
XLA Modules:
  0.0 96.6 jit_solution(2161631575693029901)
XLA Ops:
  0.7 0.7 convert_bitcast_fusion.2
  1.3 0.7 fusion.78
  2.0 0.7 maximum_bitcast_fusion.1
  2.7 0.7 fusion.60
  3.6 0.8 select_reduce_fusion
  4.4 0.7 fusion.73
  5.1 0.8 scatter_custom_fusion
  5.8 0.8 copy.61
  6.6 6.7 %all-to-all-start = ((f32[3,16,8]{2,0,1:T(4,128)}), f32[3,16,8]{2,0,1:T(4,128)S(1)}, u32[]{:S(2)}, u32[]{:S(2)}) async-start(f32[3,16,8]{2,0,1:T(4,128)} %copy.61), calls=%async_computation | async-start | bytes 65536 | tf_op jit(solution)/shard_map/all_to_all | solution.py:83
  13.3 3.5 %copy.56 = bf16[3,64,32,128]{1,3,2,0:T(8,128)(2,1)S(1)} copy(bf16[3,64,32,128]{3,2,1,0:T(8,128)(2,1)} %param.33) | data formatting | bytes 3145728 | tf_op args[0]
  16.8 0.9 convert_reduce_fusion
  17.7 0.6 copy-done
  18.4 0.6 copy-done.10
  19.0 3.8 %fusion = bf16[3,64,32,128]{1,3,2,0:T(8,128)(2,1)S(1)} fusion(bf16[3,64,32,128]{1,3,2,0:T(8,128)(2,1)} %copy-done, f32[3,32,128]{2,1,0:T(8,128)S(1)} %broadcast_multiply_fusion.4), kind=kLoop, calls=%fused_computation.10 | loop fusion | flops 2359296 | bytes 3194880 | tf_op jit(solution)/shard_map/convert_element_type | solution.py:136
  22.9 0.9 broadcast_multiply_fusion.2
  23.8 5.7 %copy.62 = bf16[3,64,32,128]{1,0,3,2:T(4,128)(2,1)} copy(bf16[3,64,32,128]{3,2,1,0:T(8,128)(2,1)} %param.33) | data formatting | bytes 3145728 | tf_op args[0]
  30.2 2.9 %gather_fusion = bf16[128,3,64]{2,1,0:T(4,128)(2,1)S(1)} fusion(bf16[3,64,4096]{1,0,2:T(4,128)(2,1)} %bitcast.196, s32[1024]{0:T(1024)S(1)} %pad_clamp_fusion.4), kind=kCustom, calls=%fused_computation | custom fusion | bytes 98816 | tf_op jit(solution)/shard_map/jit(_take)/gather | solution.py:86
  33.4 2.3 %collective-permute-start.1 = (bf16[1,1,67,128]{3,2,1,0:T(8,128)(2,1)S(1)}, bf16[1,1,67,128]{3,2,1,0:T(8,128)(2,1)S(1)}, u32[]{:S(2)}, u32[]{:S(2)}) collective-permute-start(bf16[1,1,67,128]{3,2,1,0:T(8,128)(2,1)S(1)} %pad_maximum_fusion.3), channel_id=1, source_target_pairs={{1,0},{2,1},{3,2},{4,3},{5,4},{6,5},{7,6},{8,7},{9,8},{10,9},{11,1... | collective-permute-start | bytes 51464 | tf_op jit(solution)/shard_map/ppermute | solution.py:22
  35.7 4.2 %collective-permute-start = (bf16[1,1,67,128]{3,2,1,0:T(8,128)(2,1)S(1)}, bf16[1,1,67,128]{3,2,1,0:T(8,128)(2,1)S(1)}, u32[]{:S(2)}, u32[]{:S(2)}) collective-permute-start(bf16[1,1,67,128]{3,2,1,0:T(8,128)(2,1)S(1)} %pad_maximum_fusion.3), channel_id=1, source_target_pairs={{0,1},{1,2},{2,3},{3,4},{4,5},{5,6},{6,7},{7,8},{8,9},{9,10},{10,1... | collective-permute-start | bytes 51464 | tf_op jit(solution)/shard_map/ppermute | solution.py:20
  39.9 0.6 fusion.87
  40.5 0.3 collective-permute-done
  40.8 0.7 collective-permute-start.2
  47.9 0.4 fusion.18
  48.3 0.5 fusion.36
  48.8 0.3 fusion.50
  49.0 0.3 fusion.17
  49.3 0.3 fusion.89
  49.8 0.3 fusion.16
  50.1 0.3 fusion.91
  50.4 0.3 fusion.90
  50.6 0.3 fusion.15
  50.9 0.3 fusion.93
  51.1 0.3 fusion.92
  51.4 0.3 fusion.14
  51.9 0.3 fusion.95
  52.2 0.3 fusion.13
  52.5 0.3 convolution_divide_fusion
  52.7 0.3 convolution_bitcast_fusion.4
  53.0 0.3 fusion.96
  53.6 5.1 %collective-permute-start.3 = (bf16[1,4,4096]{2,1,0:T(4,128)(2,1)S(1)}, bf16[1,4,4096]{2,1,0:T(4,128)(2,1)S(1)}, u32[]{:S(2)}, u32[]{:S(2)}) collective-permute-start(bf16[1,4,4096]{2,1,0:T(4,128)(2,1)S(1)} %reshape.538), channel_id=1, source_target_pairs={{0,1},{1,2},{2,3},{3,4},{4,5},{5,6},{6,7},{7,8},{8,9},{9,10},{10,1... | collective-permute-start | bytes 98312 | tf_op jit(solution)/shard_map/ppermute | solution.py:20
  58.8 1.9 %collective-permute-start.4 = (bf16[1,4,4096]{2,1,0:T(4,128)(2,1)S(1)}, bf16[1,4,4096]{2,1,0:T(4,128)(2,1)S(1)}, u32[]{:S(2)}, u32[]{:S(2)}) collective-permute-start(bf16[1,4,4096]{2,1,0:T(4,128)(2,1)S(1)} %reshape.538), channel_id=1, source_target_pairs={{1,0},{2,1},{3,2},{4,3},{5,4},{6,5},{7,6},{8,7},{9,8},{10,9},{11,1... | collective-permute-start | bytes 98312 | tf_op jit(solution)/shard_map/ppermute | solution.py:22
  60.7 4.1 %collective-permute-done.4 = bf16[1,4,4096]{2,1,0:T(4,128)(2,1)S(1)} collective-permute-done((bf16[1,4,4096]{2,1,0:T(4,128)(2,1)S(1)}, bf16[1,4,4096]{2,1,0:T(4,128)(2,1)S(1)}, u32[]{:S(2)}, u32[]{:S(2)}) %collective-permute-start.4) | collective-permute-done | bytes 32800 | tf_op jit(solution)/shard_map/ppermute | solution.py:22
  64.9 0.6 copy-done.5
  65.5 0.7 fusion.86
  66.3 1.3 %collective-permute-start.5 = (bf16[3,1,4096]{2,1,0:T(2,128)(2,1)}, bf16[3,1,4096]{2,1,0:T(2,128)(2,1)}, u32[]{:S(2)}, u32[]{:S(2)}) collective-permute-start(bf16[3,1,4096]{2,1,0:T(2,128)(2,1)} %get-tuple-element.60), channel_id=1, source_target_pairs={} | collective-permute-start | bytes 73736 | tf_op jit(solution)/shard_map/ppermute | solution.py:20
  67.5 1.3 %collective-permute-start.6 = (bf16[3,1,4096]{2,1,0:T(2,128)(2,1)}, bf16[3,1,4096]{2,1,0:T(2,128)(2,1)}, u32[]{:S(2)}, u32[]{:S(2)}) collective-permute-start(bf16[3,1,4096]{2,1,0:T(2,128)(2,1)} %get-tuple-element.61), channel_id=1, source_target_pairs={} | collective-permute-start | bytes 73736 | tf_op jit(solution)/shard_map/ppermute | solution.py:22
  68.8 1.0 div.97
  69.8 0.8 copy.57
  70.6 1.1 %pad_maximum_fusion = bf16[3,6,4096]{2,1,0:T(8,128)(2,1)S(1)} fusion(bf16[3,1,4096]{2,1,0:T(2,128)(2,1)} %collective-permute-done.6, bf16[3,4,4096]{2,1,0:T(4,128)(2,1)} %copy-done.5, bf16[3,1,4096]{2,1,0:T(2,128)(2,1)} %collective-permute-done.5), kind=kLoop, calls=%fused_computation.57 | loop fusion | flops 442368 | bytes 294912 | tf_op jit(solution)/shard_map/concatenate | solution.py:18
  71.8 1.0 scatter.30
  72.9 1.0 scatter.31
  73.8 1.0 %reshape.539 = bf16[3,6,64,64]{3,2,1,0:T(8,128)(2,1)} reshape(bf16[3,6,4096]{2,1,0:T(8,128)(2,1)S(1)} %scatter.31) | data formatting | bytes 294912 | tf_op jit(solution)/shard_map/reshape | solution.py:134
  74.8 1.5 %gather_fusion.4 = bf16[2,6,64,64]{3,2,1,0:T(8,128)(2,1)S(1)} fusion(bf16[3,6,64,64]{3,2,1,0:T(8,128)(2,1)} %reshape.539, s32[1024]{0:T(1024)S(1)} %get-tuple-element.81), kind=kCustom, calls=%fused_computation.4 | custom fusion | bytes 196616 | tf_op jit(solution)/shard_map/gather | solution.py:153
  76.4 1.5 %gather_fusion.1 = bf16[2,6,64,64]{3,2,1,0:T(8,128)(2,1)S(1)} fusion(bf16[3,6,64,64]{3,2,1,0:T(8,128)(2,1)} %reshape.539, s32[1024]{0:T(1024)S(1)} %get-tuple-element.84), kind=kCustom, calls=%fused_computation.1 | custom fusion | bytes 196616 | tf_op jit(solution)/shard_map/gather | solution.py:153
  77.9 1.3 %gather_fusion.2 = bf16[8,2,64,64]{3,2,1,0:T(8,128)(2,1)} fusion(bf16[2,6,64,64]{3,2,1,0:T(8,128)(2,1)S(1)} %gather_fusion.1, s32[1024]{0:T(1024)S(1)} %get-tuple-element.83), kind=kCustom, calls=%fused_computation.2 | custom fusion | bytes 262176 | tf_op jit(solution)/shard_map/gather | solution.py:153
  79.2 1.3 %gather_fusion.3 = bf16[8,2,64,64]{3,2,1,0:T(8,128)(2,1)} fusion(bf16[2,6,64,64]{3,2,1,0:T(8,128)(2,1)S(1)} %gather_fusion.1, s32[1024]{0:T(1024)S(1)} %get-tuple-element.82), kind=kCustom, calls=%fused_computation.3 | custom fusion | bytes 262176 | tf_op jit(solution)/shard_map/gather | solution.py:153
  80.5 1.3 %gather_fusion.6 = bf16[8,2,64,64]{3,2,1,0:T(8,128)(2,1)} fusion(bf16[2,6,64,64]{3,2,1,0:T(8,128)(2,1)S(1)} %gather_fusion.4, s32[1024]{0:T(1024)S(1)} %get-tuple-element.82), kind=kCustom, calls=%fused_computation.6 | custom fusion | bytes 262176 | tf_op jit(solution)/shard_map/gather | solution.py:153
  81.8 1.3 %gather_fusion.5 = bf16[8,2,64,64]{3,2,1,0:T(8,128)(2,1)} fusion(bf16[2,6,64,64]{3,2,1,0:T(8,128)(2,1)S(1)} %gather_fusion.4, s32[1024]{0:T(1024)S(1)} %get-tuple-element.83), kind=kCustom, calls=%fused_computation.5 | custom fusion | bytes 262176 | tf_op jit(solution)/shard_map/gather | solution.py:153
  83.0 1.9 %fusion.7 = f32[2,8,64,3,16,16]{2,5,4,3,1,0:T(8,128)S(1)} fusion(bf16[3,64,2,16,8,16]{1,5,4,3,2,0:T(8,128)(2,1)S(1)} %bitcast.191, bf16[8,2,64,64]{3,2,1,0:T(8,128)(2,1)} %gather_fusion.5), kind=kOutput, calls=%fused_computation.21 | convolution fusion | flops 100663296 | bytes 4849664 | tf_op jit(solution)/shard_map/fkhasb,hskm->fmhasb/dot_general | solution.py:154
  85.0 1.0 fusion.9
  86.1 1.0 fusion.11
  87.2 5.3 %fusion.2 = bf16[3,64,2,16,8,16]{1,5,3,0,4,2:T(8,128)(2,1)S(1)} fusion(f32[2,8,64,3,16,16]{2,5,4,3,1,0:T(8,128)S(1)} %fusion.7, f32[2,8,64,3,16,16]{2,5,4,3,1,0:T(8,128)S(1)} %fusion.9, f32[2,8,64,3,16,16]{2,5,4,3,1,0:T(8,128)S(1)} %fusion.11, f32[2,16,8,16]{3,1,2,0:T(8,128)S(1)} %copy-done.7, f32[2,16,8,16]{3,1,2,0:T(8,128)S(1)} %copy-done.8, ...), kind=kOutput, calls=%fused_computation.13 | convolution fusion | flops 107741184 | bytes 12828672 | tf_op jit(solution)/shard_map/fkhasb,hskm->fmhasb/dot_general | solution.py:154
  92.6 0.9 copy.74
  93.5 3.1 %copy.75 = bf16[3,64,32,128]{3,2,1,0:T(8,128)(2,1)} copy(bf16[3,64,32,128]{1,3,2,0:T(8,128)(2,1)S(1)} %bitcast.195) | data formatting | bytes 3145728 | tf_op jit(solution)/shard_map/convert_element_type | solution.py:161
  (102 shorter events, 3.9 us)
Async XLA Ops:
  6.6 23.0 %all-to-all-start = ((f32[3,16,8]{2,0,1:T(4,128)}), f32[3,16,8]{2,0,1:T(4,128)S(1)}, u32[]{:S(2)}, u32[]{:S(2)}) async-start(f32[3,16,8]{2,0,1:T(4,128)} %copy.61), calls=%async_computation | async-start | bytes 65536 | tf_op jit(solution)/shard_map/all_to_all | solution.py:83
  16.8 1.6 %copy-start = (bf16[3,64,32,128]{1,3,2,0:T(8,128)(2,1)}, bf16[3,64,32,128]{1,3,2,0:T(8,128)(2,1)S(1)}, u32[]{:S(2)}) copy-start(bf16[3,64,32,128]{1,3,2,0:T(8,128)(2,1)S(1)} %copy.56) | copy-start | bytes 4718596
  16.8 6.1 %copy-start.11 = (f32[8,16]{1,0:T(8,128)S(1)}, f32[8,16]{1,0:T(8,128)}, u32[]{:S(2)}) copy-start(f32[8,16]{1,0:T(8,128)} %constant.246) | copy-start | bytes 1540
  16.8 6.0 %copy-start.12 = (f32[8,16]{1,0:T(8,128)S(1)}, f32[8,16]{1,0:T(8,128)}, u32[]{:S(2)}) copy-start(f32[8,16]{1,0:T(8,128)} %constant.236.clone) | copy-start | bytes 1540
  16.8 6.0 %copy-start.14 = (f32[2,16]{1,0:T(2,128)S(1)}, f32[2,16]{1,0:T(2,128)}, u32[]{:S(2)}) copy-start(f32[2,16]{1,0:T(2,128)} %constant.244) | copy-start | bytes 388
  16.8 6.0 %copy-start.15 = (f32[2,16]{1,0:T(2,128)S(1)}, f32[2,16]{1,0:T(2,128)}, u32[]{:S(2)}) copy-start(f32[2,16]{1,0:T(2,128)} %constant.235.clone) | copy-start | bytes 388
  18.4 5.4 %copy-start.13 = (s32[16,4]{0,1:T(4,128)S(1)}, s32[16,4]{0,1:T(4,128)}, u32[]{:S(2)}) copy-start(s32[16,4]{0,1:T(4,128)} %param.39) | copy-start | bytes 772
  18.4 0.6 copy-start.10
  33.4 7.1 %collective-permute-start.1 = (bf16[1,1,67,128]{3,2,1,0:T(8,128)(2,1)S(1)}, bf16[1,1,67,128]{3,2,1,0:T(8,128)(2,1)S(1)}, u32[]{:S(2)}, u32[]{:S(2)}) collective-permute-start(bf16[1,1,67,128]{3,2,1,0:T(8,128)(2,1)S(1)} %pad_maximum_fusion.3), channel_id=1, source_target_pairs={{1,0},{2,1},{3,2},{4,3},{5,4},{6,5},{7,6},{8,7},{9,8},{10,9},{11,1... | collective-permute-start | bytes 51464 | tf_op jit(solution)/shard_map/ppermute | solution.py:22
  35.7 5.1 %collective-permute-start = (bf16[1,1,67,128]{3,2,1,0:T(8,128)(2,1)S(1)}, bf16[1,1,67,128]{3,2,1,0:T(8,128)(2,1)S(1)}, u32[]{:S(2)}, u32[]{:S(2)}) collective-permute-start(bf16[1,1,67,128]{3,2,1,0:T(8,128)(2,1)S(1)} %pad_maximum_fusion.3), channel_id=1, source_target_pairs={{0,1},{1,2},{2,3},{3,4},{4,5},{5,6},{6,7},{7,8},{8,9},{9,10},{10,1... | collective-permute-start | bytes 51464 | tf_op jit(solution)/shard_map/ppermute | solution.py:20
  40.8 5.7 %collective-permute-start.2 = (bf16[3,1,67,128]{3,2,1,0:T(8,128)(2,1)S(1)}, bf16[3,1,67,128]{3,2,1,0:T(8,128)(2,1)S(1)}, u32[]{:S(2)}, u32[]{:S(2)}) collective-permute-start(bf16[3,1,67,128]{3,2,1,0:T(8,128)(2,1)S(1)} %pad_maximum_fusion.2), channel_id=1, source_target_pairs={} | collective-permute-start | bytes 154376 | tf_op jit(solution)/shard_map/ppermute | solution.py:20
  47.5 11.2 %copy-start.18 = (s32[8]{0:T(128)S(1)}, s32[8]{0:T(128)}, u32[]{:S(2)}) copy-start(s32[8]{0:T(128)} %constant.250) | copy-start | bytes 100
  47.7 21.1 %copy-start.16 = (s32[2]{0:T(128)S(1)}, s32[2]{0:T(128)}, u32[]{:S(2)}) copy-start(s32[2]{0:T(128)} %constant.252) | copy-start | bytes 28
  47.7 21.1 %copy-start.17 = (s32[8]{0:T(128)S(1)}, s32[8]{0:T(128)}, u32[]{:S(2)}) copy-start(s32[8]{0:T(128)} %constant.251) | copy-start | bytes 100
  53.6 7.1 %collective-permute-start.3 = (bf16[1,4,4096]{2,1,0:T(4,128)(2,1)S(1)}, bf16[1,4,4096]{2,1,0:T(4,128)(2,1)S(1)}, u32[]{:S(2)}, u32[]{:S(2)}) collective-permute-start(bf16[1,4,4096]{2,1,0:T(4,128)(2,1)S(1)} %reshape.538), channel_id=1, source_target_pairs={{0,1},{1,2},{2,3},{3,4},{4,5},{5,6},{6,7},{7,8},{8,9},{9,10},{10,1... | collective-permute-start | bytes 98312 | tf_op jit(solution)/shard_map/ppermute | solution.py:20
  58.8 6.1 %collective-permute-start.4 = (bf16[1,4,4096]{2,1,0:T(4,128)(2,1)S(1)}, bf16[1,4,4096]{2,1,0:T(4,128)(2,1)S(1)}, u32[]{:S(2)}, u32[]{:S(2)}) collective-permute-start(bf16[1,4,4096]{2,1,0:T(4,128)(2,1)S(1)} %reshape.538), channel_id=1, source_target_pairs={{1,0},{2,1},{3,2},{4,3},{5,4},{6,5},{7,6},{8,7},{9,8},{10,9},{11,1... | collective-permute-start | bytes 98312 | tf_op jit(solution)/shard_map/ppermute | solution.py:22
  64.9 0.6 copy-start.5
  66.3 4.3 %collective-permute-start.5 = (bf16[3,1,4096]{2,1,0:T(2,128)(2,1)}, bf16[3,1,4096]{2,1,0:T(2,128)(2,1)}, u32[]{:S(2)}, u32[]{:S(2)}) collective-permute-start(bf16[3,1,4096]{2,1,0:T(2,128)(2,1)} %get-tuple-element.60), channel_id=1, source_target_pairs={} | collective-permute-start | bytes 73736 | tf_op jit(solution)/shard_map/ppermute | solution.py:20
  67.5 3.1 %collective-permute-start.6 = (bf16[3,1,4096]{2,1,0:T(2,128)(2,1)}, bf16[3,1,4096]{2,1,0:T(2,128)(2,1)}, u32[]{:S(2)}, u32[]{:S(2)}) collective-permute-start(bf16[3,1,4096]{2,1,0:T(2,128)(2,1)} %get-tuple-element.61), channel_id=1, source_target_pairs={} | collective-permute-start | bytes 73736 | tf_op jit(solution)/shard_map/ppermute | solution.py:22
  83.0 2.0 %copy-start.4 = (bf16[8,2,64,64]{3,2,1,0:T(8,128)(2,1)S(1)}, bf16[8,2,64,64]{3,2,1,0:T(8,128)(2,1)}, u32[]{:S(2)}) copy-start(bf16[8,2,64,64]{3,2,1,0:T(8,128)(2,1)} %gather_fusion.3) | copy-start | bytes 393220
  85.0 1.0 %copy-start.3 = (bf16[8,2,64,64]{3,2,1,0:T(8,128)(2,1)S(1)}, bf16[8,2,64,64]{3,2,1,0:T(8,128)(2,1)}, u32[]{:S(2)}) copy-start(bf16[8,2,64,64]{3,2,1,0:T(8,128)(2,1)} %gather_fusion.2) | copy-start | bytes 393220
  86.0 1.0 %copy-start.1 = (f32[3,2,16,8,16]{4,2,0,3,1:T(8,128)S(1)}, f32[3,2,16,8,16]{4,2,0,3,1:T(8,128)}, u32[]{:S(2)}) copy-start(f32[3,2,16,8,16]{4,2,0,3,1:T(8,128)} %copy.57) | copy-start | bytes 147460
  86.0 1.1 %copy-start.2 = (bf16[8,2,64,64]{3,2,1,0:T(8,128)(2,1)S(1)}, bf16[8,2,64,64]{3,2,1,0:T(8,128)(2,1)}, u32[]{:S(2)}) copy-start(bf16[8,2,64,64]{3,2,1,0:T(8,128)(2,1)} %gather_fusion.6) | copy-start | bytes 393220
  86.0 1.1 %copy-start.6 = (f32[2,16,8,16]{3,1,2,0:T(8,128)S(1)}, f32[2,16,8,16]{3,1,2,0:T(8,128)}, u32[]{:S(2)}) copy-start(f32[2,16,8,16]{3,1,2,0:T(8,128)} %get-tuple-element.69) | copy-start | bytes 49156
  86.0 1.1 %copy-start.7 = (f32[2,16,8,16]{3,1,2,0:T(8,128)S(1)}, f32[2,16,8,16]{3,1,2,0:T(8,128)}, u32[]{:S(2)}) copy-start(f32[2,16,8,16]{3,1,2,0:T(8,128)} %get-tuple-element.70) | copy-start | bytes 49156
  86.0 1.1 %copy-start.8 = (f32[2,16,8,16]{3,1,2,0:T(8,128)S(1)}, f32[2,16,8,16]{3,1,2,0:T(8,128)}, u32[]{:S(2)}) copy-start(f32[2,16,8,16]{3,1,2,0:T(8,128)} %get-tuple-element.71) | copy-start | bytes 49156
  86.0 1.2 %copy-start.9 = (f32[2,16,8,16]{3,1,2,0:T(8,128)S(1)}, f32[2,16,8,16]{3,1,2,0:T(8,128)}, u32[]{:S(2)}) copy-start(f32[2,16,8,16]{3,1,2,0:T(8,128)} %get-tuple-element.72) | copy-start | bytes 49156
where the time goes:
time: 97.4 us; the launch traced here: 96.6 us
  local copies, waits for them, and re-layouts  35.4 us (36%)
  starting transfers between devices  23.3 us (24%)
  matrix products  15.3 us (16%)
  other arithmetic  11.8 us (12%)
  between operations  6.33 us (6%)
  waiting for transfers between devices  4.44 us (5%)
    unnamed x46, local copies, waits for them, and re-layouts  11.4 us
    ppermute x4, starting transfers between devices, with_halo(): lax.ppermute(tail, axis, [(i, (i + 1) % count) for i in range(ends)])  11.2 us
    dot_general x4, matrix products, body(): jnp.einsum('fkhasb,hskm->fmhasb', pieces, corner, preferred_element_type=...  9.2 us
    gather x6, local copies, waits for them, and re-layouts, body(): corner = framed[upper_index + down_step][:, left_index + right_step]  8.21 us
    all_to_all x1, starting transfers between devices, body(): lax.all_to_all(outgoing, 'gy', split_axis=1, concat_axis=1, tiled=True)  6.67 us
    ppermute x3, starting transfers between devices, with_halo(): lax.ppermute(head, axis, [((i + 1) % count, i) for i in range(ends)])  5.45 us
    ppermute x3, waiting for transfers between devices, with_halo(): lax.ppermute(head, axis, [((i + 1) % count, i) for i in range(ends)])  4.15 us
    convert_element_type x2, local copies, waits for them, and re-layouts, body(): analysis.reshape(fields, members, tile_rows, tile_cols).astype(jnp.bfloat16)  4.01 us
  transfers between devices with their start and end apart: 8, of which 2 were waited for; matrix products, arithmetic and copies ran while one was open for 18% of the time, Pallas kernels for 0%

commit v1 on v0

--- a/solution.py
+++ b/solution.py
@@ -2,6 +2,8 @@
 import jax.numpy as jnp
 import numpy as np
 from jax import lax
+from jax.experimental import pallas as pl
+from jax.experimental.pallas import tpu as pltpu
 from jax.sharding import PartitionSpec as P
 
 STRIDE = 32
@@ -161,6 +163,347 @@
     return analysis.reshape(fields, members, tile_rows, tile_cols).astype(jnp.bfloat16)
 
 
+MEMBERS = 64
+ROWS = 32
+COLS = 128
+POINTS = 4
+CAPACITY = 2 * OBS_PEER
+PACK = 80
+NT = (((1,), (1,)), ((), ()))
+NN = (((1,), (0,)), ((), ()))
+
+
+def dot(a, b, dims=NN, precision=None):
+    return lax.dot_general(
+        a, b, dims, precision=precision, preferred_element_type=jnp.float32
+    )
+
+
+def iota(shape, dim):
+    return lax.broadcasted_iota(jnp.int32, shape, dim)
+
+
+def split_high_low(x):
+    high = x.astype(jnp.bfloat16)
+    low = (x - high.astype(jnp.float32)).astype(jnp.bfloat16)
+    return high, low
+
+
+def pair_matmul(a, b, block_mask):
+    a_high, a_low = split_high_low(a)
+    diagonal = jnp.where(block_mask, jnp.concatenate([b, b], axis=0), 0.0)
+    b_high, b_low = split_high_low(diagonal)
+    return dot(a_high, b_high) + (dot(a_high, b_low) + dot(a_low, b_high))
+
+
+def solve_pair(gram, forcing):
+    shape = (MEMBERS, 2 * MEMBERS)
+    identity = jnp.where(iota(shape, 0) == iota(shape, 1) % MEMBERS, 1.0, 0.0)
+    square = (2 * MEMBERS, 2 * MEMBERS)
+    block_mask = (iota(square, 0) < MEMBERS) == (iota(square, 1) < MEMBERS)
+    left = iota((1, 2 * MEMBERS), 1) < MEMBERS
+    matrix = identity + gram / (MEMBERS - 1.0)
+    sums = jnp.sum(matrix * matrix, axis=0, keepdims=True)
+    left_sum = jnp.sum(jnp.where(left, sums, 0.0), axis=1, keepdims=True)
+    right_sum = jnp.sum(jnp.where(left, 0.0, sums), axis=1, keepdims=True)
+    norm_scale = jnp.sqrt(jnp.where(left, left_sum, right_sum))
+    current = matrix / norm_scale
+    factor = 1.5 * identity - 0.5 * current
+    inverse_root = factor
+    current = pair_matmul(current, factor, block_mask)
+    for iteration in range(1, ITER_NS):
+        factor = 1.5 * identity - 0.5 * pair_matmul(inverse_root, current, block_mask)
+        if iteration < ITER_NS - 1:
+            current = pair_matmul(current, factor, block_mask)
+        inverse_root = pair_matmul(factor, inverse_root, block_mask)
+    square_root = inverse_root / jnp.sqrt(norm_scale)
+    row = jnp.broadcast_to(forcing, (8, 2 * MEMBERS))
+    shift = pair_matmul(pair_matmul(row, square_root, block_mask), square_root, block_mask)
+    return (square_root + shift[0:1] / (MEMBERS - 1.0)).astype(jnp.bfloat16)
+
+
+def kernel(
+    peers,
+    state_hbm, value_ref, sigma_ref, pixel_ref, route_ref, count_ref, radius_ref,
+    out_hbm,
+    state_v, wide, mixed, total, centres, outbox, inbox, picked, pack_own, pack_halo,
+    weight_own, weight_halo, result,
+    state_sem, out_sem, send_sem, recv_sem, pack_send, pack_recv, weight_send, weight_recv,
+):
+    group = lax.axis_index("groups")
+    me = lax.axis_index("gy")
+    fields = state_hbm.shape[0] // MEMBERS
+    span = MEMBERS * ROWS
+
+    def at(target):
+        return (group, target, 0)
+
+    load = pltpu.make_async_copy(state_hbm, state_v, state_sem)
+    load.start()
+    barrier = pltpu.get_barrier_semaphore()
+
+    @pl.loop(1, peers)
+    def _(step):
+        pl.semaphore_signal(
+            barrier, inc=1, device_id=at(lax.rem(me + step, peers)),
+            device_id_type=pl.DeviceIdType.MESH,
+        )
+
+    arrivals = value_ref.shape[1]
+    route = route_ref[...]
+    present = iota((1, arrivals), 1) < count_ref[...]
+    inverse_sigma = jnp.where(present, 1.0 / sigma_ref[...], 0.0)
+    pixel = pixel_ref[...].astype(jnp.float32)
+    kind = iota((8, arrivals), 0)
+    record = jnp.where(
+        kind == 0, value_ref[...],
+        jnp.where(kind == 1, inverse_sigma, jnp.where(kind == 2, pixel, 0.0)),
+    )
+    hot = jnp.where(iota((peers, arrivals), 0) == route, 1.0, 0.0)
+    earlier = jnp.where(iota((arrivals, arrivals), 0) < iota((arrivals, arrivals), 1), 1.0, 0.0)
+    counted = dot(hot.astype(jnp.bfloat16), earlier.astype(jnp.bfloat16))
+    rank = jnp.sum(counted * hot, axis=0, keepdims=True).astype(jnp.int32)
+    place = jnp.where(iota((COLS, arrivals), 0) == rank + me * CAPACITY, 1.0, 0.0)
+    routed = jnp.concatenate(
+        [jnp.where(route == target, record, 0.0) for target in range(peers)], axis=0
+    )
+    outbox[...] = dot(routed, place, NT, lax.Precision.HIGHEST)
+    own = pl.ds(pl.multiple_of(me * 8, 8), 8)
+
+    @pl.when(me == 0)
+    def _():
+        pack_halo[0] = jnp.zeros((PACK, COLS), jnp.bfloat16)
+
+    @pl.when(me == peers - 1)
+    def _():
+        pack_halo[1] = jnp.zeros((PACK, COLS), jnp.bfloat16)
+
+    pl.semaphore_wait(barrier, peers - 1)
+
+    def obs_copy(step):
+        target = lax.rem(me + step, peers)
+        return pltpu.make_async_remote_copy(
+            src_ref=outbox.at[pl.ds(pl.multiple_of(target * 8, 8), 8)],
+            dst_ref=inbox.at[own],
+            send_sem=send_sem.at[step],
+            recv_sem=recv_sem.at[step],
+            device_id=at(target),
+            device_id_type=pl.DeviceIdType.MESH,
+        )
+
+    @pl.loop(1, peers)
+    def _(step):
+        obs_copy(step).start()
+
+    inbox[own, :] = outbox[own, :]
+    load.wait()
+
+    for field in range(fields):
+        @pl.loop(0, 8)
+        def _(chunk):
+            first = pl.multiple_of(field * span + chunk * 256, 256)
+            members = field * MEMBERS + chunk * 8
+            wide[pl.ds(first, 256), :] = (
+                state_v[pl.ds(members, 8)].astype(jnp.float32).reshape(256, COLS)
+            )
+
+    column = iota((1, COLS), 1)
+    position = (column - STRIDE // 2).astype(jnp.float32) / STRIDE
+    position = jnp.clip(position, 0.0, POINTS - 1.0)
+    hats = [
+        jnp.maximum(1.0 - jnp.abs(position - point), 0.0).astype(jnp.bfloat16)
+        for point in range(POINTS)
+    ]
+
+    @pl.loop(0, ROWS)
+    def _(row):
+        for field in range(fields):
+            cells = wide[pl.ds(field * span + row, MEMBERS, ROWS), :]
+            centre = jnp.sum(cells, axis=0, keepdims=True) * (1.0 / MEMBERS)
+            lanes = slice(field * COLS, (field + 1) * COLS)
+            centres[row, :, lanes] = centre
+            anomaly = (cells - centre).astype(jnp.bfloat16)
+            for point in range(POINTS):
+                mixed[row, point * MEMBERS:(point + 1) * MEMBERS, lanes] = anomaly * hats[point]
+
+    @pl.loop(1, peers)
+    def _(step):
+        obs_copy(step).wait()
+
+    arrived = jnp.sum(inbox[...].reshape(peers, 8, COLS), axis=0)
+    value, weight = arrived[0:1], arrived[1:2]
+    pixels = arrived[2:3].astype(jnp.int32)
+    obs_row, obs_col = pixels // COLS, pixels % COLS
+    col_hot = jnp.where(iota((COLS, COLS), 0) == obs_col, 1.0, 0.0).astype(jnp.bfloat16)
+    row_hot = jnp.where(iota((ROWS, COLS), 0) == obs_row, 1.0, 0.0)
+    for part in range(fields * 2):
+        block = state_v[part * 32:(part + 1) * 32].reshape(32 * ROWS, COLS)
+        found = dot(block, col_hot).reshape(32, ROWS, COLS) * row_hot
+        picked[part * 32:(part + 1) * 32, :] = jnp.sum(found, axis=1)
+    thickness, temperature, crust = (
+        picked[field * MEMBERS:(field + 1) * MEMBERS, :] for field in range(fields)
+    )
+    predicted = temperature * jax.nn.sigmoid(thickness) - 0.5 * crust
+    centre = jnp.mean(predicted, axis=0, keepdims=True)
+    pack_own[0:MEMBERS, :] = ((predicted - centre) * weight).astype(jnp.bfloat16)
+    kind = iota((PACK - MEMBERS, COLS), 0)
+    pack_own[MEMBERS:PACK, :] = jnp.where(
+        kind == 0, (value - centre) * weight,
+        jnp.where(
+            kind == 1, obs_row.astype(jnp.float32),
+            jnp.where(kind == 2, obs_col.astype(jnp.float32), 0.0),
+        ),
+    ).astype(jnp.bfloat16)
+
+    def halo_copy(source, slots, send, recv, down):
+        return pltpu.make_async_remote_copy(
+            src_ref=source,
+            dst_ref=slots.at[0 if down else 1],
+            send_sem=send.at[0 if down else 1],
+            recv_sem=recv.at[0 if down else 1],
+            device_id=at(me + 1 if down else me - 1),
+            device_id_type=pl.DeviceIdType.MESH,
+        )
+
+    def exchange(source, slots, send, recv):
+        @pl.when(me < peers - 1)
+        def _():
+            halo_copy(source, slots, send, recv, True).start()
+
+        @pl.when(me > 0)
+        def _():
+            halo_copy(source, slots, send, recv, False).start()
+
+    def finish(source, slots, send, recv):
+        @pl.when(me < peers - 1)
+        def _():
+            halo_copy(source, slots, send, recv, True).wait_send()
+            halo_copy(source, slots, send, recv, False).wait_recv()
+
+        @pl.when(me > 0)
+        def _():
+            halo_copy(source, slots, send, recv, False).wait_send()
+            halo_copy(source, slots, send, recv, True).wait_recv()
+
+    exchange(pack_own, pack_halo, pack_send, pack_recv)
+    radii = [radius_ref[me, point].astype(jnp.float32) for point in range(POINTS)]
+
+    def tile_gram(pack, offset):
+        spread = pack[0:MEMBERS]
+        wider = pack.astype(jnp.float32)
+        near_row = wider[MEMBERS + 1:MEMBERS + 2] + (offset * ROWS - STRIDE // 2)
+        near_col = wider[MEMBERS + 2:MEMBERS + 3]
+        scaled = []
+        forced = []
+        for point in range(POINTS):
+            nearness = taper_weight(
+                near_row, near_col - (STRIDE * point + STRIDE // 2), radii[point]
+            )
+            scaled.append((nearness * wider[0:MEMBERS]).astype(jnp.bfloat16))
+            forced.append(nearness * wider[MEMBERS:MEMBERS + 1])
+        forced = jnp.concatenate(forced + forced, axis=0).astype(jnp.bfloat16)
+        gram = dot(spread, jnp.concatenate(scaled, axis=0), NT)
+        forcing = dot(forced, jnp.concatenate([spread, spread], axis=0), NT)
+        return gram, forcing
+
+    gram, forcing = tile_gram(pack_own[...], 0)
+    finish(pack_own, pack_halo, pack_send, pack_recv)
+    for slot, offset in ((0, -1), (1, 1)):
+        more_gram, more_forcing = tile_gram(pack_halo[slot], offset)
+        gram, forcing = gram + more_gram, forcing + more_forcing
+    left = iota((1, 2 * MEMBERS), 1) < MEMBERS
+    for pair in range(POINTS // 2):
+        lanes = slice(pair * 2 * MEMBERS, (pair + 1) * 2 * MEMBERS)
+        rows = jnp.where(left, forcing[2 * pair:2 * pair + 1], forcing[2 * pair + 1:2 * pair + 2])
+        weight_own[:, lanes] = solve_pair(gram[:, lanes], rows)
+    exchange(weight_own, weight_halo, weight_send, weight_recv)
+
+    half = ROWS // 2
+
+    @pl.loop(0, ROWS)
+    def _(row):
+        fraction = (half + jnp.minimum(row, ROWS - row)).astype(jnp.float32) / STRIDE
+        product = dot(weight_own[...], mixed[row])
+        total[row] = centres[row] + fraction * product
+
+    finish(weight_own, weight_halo, weight_send, weight_recv)
+
+    @pl.when(me == 0)
+    def _():
+        weight_halo[0] = weight_own[...]
+
+    @pl.when(me == peers - 1)
+    def _():
+        weight_halo[1] = weight_own[...]
+
+    @pl.loop(0, ROWS)
+    def _(row):
+        fraction = (half - jnp.minimum(row, ROWS - row)).astype(jnp.float32) / STRIDE
+        product = dot(weight_halo[row // half], mixed[row])
+        done = total[row] + fraction * product
+        for field in range(fields):
+            wide[pl.ds(field * span + row, MEMBERS, ROWS), :] = (
+                done[:, field * COLS:(field + 1) * COLS]
+            )
+
+    for field in range(fields):
+        @pl.loop(0, 8)
+        def _(chunk):
+            first = pl.multiple_of(field * span + chunk * 256, 256)
+            members = field * MEMBERS + chunk * 8
+            result[pl.ds(members, 8)] = (
+                wide[pl.ds(first, 256), :].astype(jnp.bfloat16).reshape(8, ROWS, COLS)
+            )
+
+    store = pltpu.make_async_copy(result, out_hbm, out_sem)
+    store.start()
+    store.wait()
+
+
+def fused_body(state, obs_value, obs_sigma, obs_pixel, obs_route, obs_count, radius):
+    fields, members, tile_rows, tile_cols = state.shape
+    peers = lax.axis_size("gy")
+    arrivals = obs_value.shape[0]
+    planes = fields * members
+    anywhere = pl.BlockSpec(memory_space=pl.ANY)
+    local = pl.BlockSpec(memory_space=pltpu.VMEM)
+    dma = pltpu.SemaphoreType.DMA
+    analysis = pl.pallas_call(
+        lambda *refs: kernel(peers, *refs),
+        out_shape=jax.ShapeDtypeStruct((planes, tile_rows, tile_cols), jnp.bfloat16),
+        in_specs=[anywhere] + [local] * 5 + [pl.BlockSpec(memory_space=pltpu.SMEM)],
+        out_specs=anywhere,
+        scratch_shapes=[
+            pltpu.VMEM((planes, tile_rows, tile_cols), jnp.bfloat16),
+            pltpu.VMEM((planes * tile_rows, tile_cols), jnp.float32),
+            pltpu.VMEM((tile_rows, POINTS * members, fields * tile_cols), jnp.bfloat16),
+            pltpu.VMEM((tile_rows, members, fields * tile_cols), jnp.float32),
+            pltpu.VMEM((tile_rows, 1, fields * tile_cols), jnp.float32),
+            pltpu.VMEM((peers * 8, tile_cols), jnp.float32),
+            pltpu.VMEM((peers * 8, tile_cols), jnp.float32),
+            pltpu.VMEM((planes, tile_cols), jnp.float32),
+            pltpu.VMEM((PACK, tile_cols), jnp.bfloat16),
+            pltpu.VMEM((2, PACK, tile_cols), jnp.bfloat16),
+            pltpu.VMEM((members, POINTS * members), jnp.bfloat16),
+            pltpu.VMEM((2, members, POINTS * members), jnp.bfloat16),
+            pltpu.VMEM((planes, tile_rows, tile_cols), jnp.bfloat16),
+            dma, dma, dma((peers,)), dma((peers,)), dma((2,)), dma((2,)), dma((2,)), dma((2,)),
+        ],
+        compiler_params=pltpu.CompilerParams(
+            collective_id=0, has_side_effects=True, vmem_limit_bytes=40 * 1024 * 1024
+        ),
+    )(
+        state.reshape(planes, tile_rows, tile_cols),
+        obs_value.reshape(1, arrivals),
+        obs_sigma.reshape(1, arrivals),
+        obs_pixel.reshape(1, arrivals),
+        obs_route.reshape(1, arrivals),
+        obs_count.reshape(1, 1),
+        radius,
+    )
+    return analysis.reshape(state.shape)
+
+
 def solution(mesh):
     placed = (
         P("groups", None, "gy", "gx"),
@@ -171,6 +514,8 @@
         P(("groups", "gy", "gx")),
         P("groups", None),
     )
+    slots = CAPACITY * mesh.shape["gy"]
+    fits = mesh.shape["gx"] == 1 and slots == COLS
     return jax.shard_map(
-        body, mesh=mesh, in_specs=placed, out_specs=P("groups", None, "gy", "gx"), check_vma=False
-    )
+        fused_body if fits else body, mesh=mesh, in_specs=placed, out_specs=P("groups", None, "gy", "gx"), check_vma=False
+    )

time: 97.4 us -> 38.9 us (0.40)
  the two profiles are of different devices: /device:TPU:3 before, /device:TPU:1 now
where the time goes in v1:
time: 38.9 us; the launch traced here: 38.7 us
  Pallas kernels  32.1 us (83%)
  local copies, waits for them, and re-layouts  5.93 us (15%)
  between operations  0.67 us (2%)
    pallas_call x1, Pallas kernels, fused_body(): pl.pallas_call(lambda *refs: kernel(peers, *refs), out_shape=jax.ShapeDty...  32.1 us
    unnamed x12, local copies, waits for them, and re-layouts  5.93 us

profile of v1, /device:TPU:1, one launch (start us, length us, event | category | flops | bytes accessed | tf_op | source)
XLA Modules:
  0.0 38.7 jit_solution(11102555575986167152)
XLA Ops:
  0.7 0.8 %copy.8.refs_6_ = s32[16,4]{1,0:T(8,128)S(1)} copy(s32[16,4]{0,1:T(4,128)} %param.13) | data formatting | bytes 512 | tf_op args[6]
  1.4 0.0 copy-start
  1.4 1.4 %copy-done = bf16[3,64,32,128]{3,2,1,0:T(8,128)(2,1)S(1)} copy-done((bf16[3,64,32,128]{3,2,1,0:T(8,128)(2,1)S(1)}, bf16[3,64,32,128]{3,2,1,0:T(8,128)(2,1)}, u32[]{:S(2)}) %copy-start) | copy-done | bytes 1572888
  2.8 0.0 copy-start.1
  2.8 0.7 %copy-done.1 = f32[64]{0:T(128)S(1)} copy-done((f32[64]{0:T(128)S(1)}, f32[64]{0:T(128)}, u32[]{:S(2)}) %copy-start.1) | copy-done | bytes 280
  3.5 0.0 copy-start.2
  3.5 0.7 %copy-done.2 = f32[64]{0:T(128)S(1)} copy-done((f32[64]{0:T(128)S(1)}, f32[64]{0:T(128)}, u32[]{:S(2)}) %copy-start.2) | copy-done | bytes 280
  4.1 0.0 copy-start.3
  4.1 0.7 %copy-done.3 = s32[64]{0:T(128)S(1)} copy-done((s32[64]{0:T(128)S(1)}, s32[64]{0:T(128)}, u32[]{:S(2)}) %copy-start.3) | copy-done | bytes 280
  4.8 0.0 copy-start.4
  4.8 0.7 %copy-done.4 = s32[64,1]{0,1:T(1,128)S(1)} copy-done((s32[64,1]{0,1:T(1,128)S(1)}, s32[64,1]{0,1:T(1,128)}, u32[]{:S(2)}) %copy-start.4) | copy-done | bytes 280
  5.4 32.1 %shard_map.73 = bf16[192,32,128]{2,1,0:T(8,128)(2,1)S(1)} custom-call(bf16[192,32,128]{2,1,0:T(8,128)(2,1)S(1)} %bitcast.9, f32[1,64]{1,0:T(1,128)S(1)} %bitcast.10, f32[1,64]{1,0:T(1,128)S(1)} %bitcast.11, s32[1,64]{1,0:T(1,128)S(1)} %bitcast.12, s32[1,64]{1,0:T(1,128)S(1)} %bitcast.13, s32[1,1]{1,0:T(1,128)} %bitcast.7.refs_5_, s32[16,4]{1,0:T(8,128)S(1)} %copy.8.refs_6_), custom_call_target="tpu_custom_call" | custom-call | tf_op jit(solution)/shard_map/pallas_call | solution.py:471
  37.6 1.1 %copy.11 = bf16[3,64,32,128]{3,2,1,0:T(8,128)(2,1)} copy(bf16[3,64,32,128]{3,2,1,0:T(8,128)(2,1)S(1)} %bitcast.8) | data formatting | bytes 3145728
Async XLA Ops:
  1.4 1.4 %copy-start = (bf16[3,64,32,128]{3,2,1,0:T(8,128)(2,1)S(1)}, bf16[3,64,32,128]{3,2,1,0:T(8,128)(2,1)}, u32[]{:S(2)}) copy-start(bf16[3,64,32,128]{3,2,1,0:T(8,128)(2,1)} %param.7) | copy-start | bytes 4718596
  2.8 0.7 %copy-start.1 = (f32[64]{0:T(128)S(1)}, f32[64]{0:T(128)}, u32[]{:S(2)}) copy-start(f32[64]{0:T(128)} %param.8) | copy-start | bytes 772
  3.5 0.7 %copy-start.2 = (f32[64]{0:T(128)S(1)}, f32[64]{0:T(128)}, u32[]{:S(2)}) copy-start(f32[64]{0:T(128)} %param.9) | copy-start | bytes 772
  4.1 0.7 %copy-start.3 = (s32[64]{0:T(128)S(1)}, s32[64]{0:T(128)}, u32[]{:S(2)}) copy-start(s32[64]{0:T(128)} %param.10) | copy-start | bytes 772
  4.8 0.7 %copy-start.4 = (s32[64,1]{0,1:T(1,128)S(1)}, s32[64,1]{0,1:T(1,128)}, u32[]{:S(2)}) copy-start(s32[64,1]{0,1:T(1,128)} %param.11) | copy-start | bytes 772

commit v2 on v1

--- a/solution.py
+++ b/solution.py
@@ -224,8 +224,9 @@
 
 def kernel(
     peers,
-    state_hbm, value_ref, sigma_ref, pixel_ref, route_ref, count_ref, radius_ref,
+    state_hbm, value_hbm, sigma_hbm, pixel_hbm, route_hbm, count_hbm, radius_hbm,
     out_hbm,
+    value_ref, sigma_ref, pixel_ref, route_ref, count_ref, radius_ref, small_sem,
     state_v, wide, mixed, total, centres, outbox, inbox, picked, pack_own, pack_halo,
     weight_own, weight_halo, result,
     state_sem, out_sem, send_sem, recv_sem, pack_send, pack_recv, weight_send, weight_recv,
@@ -239,6 +240,15 @@
         return (group, target, 0)
 
     load = pltpu.make_async_copy(state_hbm, state_v, state_sem)
+    small = [
+        pltpu.make_async_copy(source, target, small_sem.at[index])
+        for index, (source, target) in enumerate((
+            (value_hbm, value_ref), (sigma_hbm, sigma_ref), (pixel_hbm, pixel_ref),
+            (route_hbm, route_ref), (count_hbm, count_ref), (radius_hbm, radius_ref),
+        ))
+    ]
+    for copy in small:
+        copy.start()
     load.start()
     barrier = pltpu.get_barrier_semaphore()
 
@@ -249,6 +259,8 @@
             device_id_type=pl.DeviceIdType.MESH,
         )
 
+    for copy in small:
+        copy.wait()
     arrivals = value_ref.shape[1]
     route = route_ref[...]
     present = iota((1, arrivals), 1) < count_ref[...]
@@ -278,6 +290,17 @@
     def _():
         pack_halo[1] = jnp.zeros((PACK, COLS), jnp.bfloat16)
 
+    load.wait()
+
+    for field in range(fields):
+        @pl.loop(0, 8, unroll=2)
+        def _(chunk):
+            first = pl.multiple_of(field * span + chunk * 256, 256)
+            members = field * MEMBERS + chunk * 8
+            wide[pl.ds(first, 256), :] = (
+                state_v[pl.ds(members, 8)].astype(jnp.float32).reshape(256, COLS)
+            )
+
     pl.semaphore_wait(barrier, peers - 1)
 
     def obs_copy(step):
@@ -296,16 +319,6 @@
         obs_copy(step).start()
 
     inbox[own, :] = outbox[own, :]
-    load.wait()
-
-    for field in range(fields):
-        @pl.loop(0, 8)
-        def _(chunk):
-            first = pl.multiple_of(field * span + chunk * 256, 256)
-            members = field * MEMBERS + chunk * 8
-            wide[pl.ds(first, 256), :] = (
-                state_v[pl.ds(members, 8)].astype(jnp.float32).reshape(256, COLS)
-            )
 
     column = iota((1, COLS), 1)
     position = (column - STRIDE // 2).astype(jnp.float32) / STRIDE
@@ -315,8 +328,7 @@
         for point in range(POINTS)
     ]
 
-    @pl.loop(0, ROWS)
-    def _(row):
+    def mix(row):
         for field in range(fields):
             cells = wide[pl.ds(field * span + row, MEMBERS, ROWS), :]
             centre = jnp.sum(cells, axis=0, keepdims=True) * (1.0 / MEMBERS)
@@ -325,6 +337,8 @@
             anomaly = (cells - centre).astype(jnp.bfloat16)
             for point in range(POINTS):
                 mixed[row, point * MEMBERS:(point + 1) * MEMBERS, lanes] = anomaly * hats[point]
+
+    pl.loop(0, ROWS // 2, unroll=4)(mix)
 
     @pl.loop(1, peers)
     def _(step):
@@ -386,27 +400,28 @@
             halo_copy(source, slots, send, recv, True).wait_recv()
 
     exchange(pack_own, pack_halo, pack_send, pack_recv)
-    radii = [radius_ref[me, point].astype(jnp.float32) for point in range(POINTS)]
+    own_column = iota(radius_ref.shape, 1) == me
+    radii = jnp.sum(jnp.where(own_column, radius_ref[...].astype(jnp.float32), 0.0), axis=1, keepdims=True)
+    point_col = (iota((POINTS, 1), 0) * STRIDE + STRIDE // 2).astype(jnp.float32)
 
     def tile_gram(pack, offset):
         spread = pack[0:MEMBERS]
         wider = pack.astype(jnp.float32)
         near_row = wider[MEMBERS + 1:MEMBERS + 2] + (offset * ROWS - STRIDE // 2)
         near_col = wider[MEMBERS + 2:MEMBERS + 3]
-        scaled = []
-        forced = []
-        for point in range(POINTS):
-            nearness = taper_weight(
-                near_row, near_col - (STRIDE * point + STRIDE // 2), radii[point]
-            )
-            scaled.append((nearness * wider[0:MEMBERS]).astype(jnp.bfloat16))
-            forced.append(nearness * wider[MEMBERS:MEMBERS + 1])
-        forced = jnp.concatenate(forced + forced, axis=0).astype(jnp.bfloat16)
+        nearness = taper_weight(near_row, near_col - point_col, radii)
+        scaled = [
+            (nearness[point:point + 1] * wider[0:MEMBERS]).astype(jnp.bfloat16)
+            for point in range(POINTS)
+        ]
+        forced = nearness * wider[MEMBERS:MEMBERS + 1]
+        forced = jnp.concatenate([forced, forced], axis=0).astype(jnp.bfloat16)
         gram = dot(spread, jnp.concatenate(scaled, axis=0), NT)
         forcing = dot(forced, jnp.concatenate([spread, spread], axis=0), NT)
         return gram, forcing
 
     gram, forcing = tile_gram(pack_own[...], 0)
+    pl.loop(ROWS // 2, ROWS, unroll=4)(mix)
     finish(pack_own, pack_halo, pack_send, pack_recv)
     for slot, offset in ((0, -1), (1, 1)):
         more_gram, more_forcing = tile_gram(pack_halo[slot], offset)
@@ -420,7 +435,7 @@
 
     half = ROWS // 2
 
-    @pl.loop(0, ROWS)
+    @pl.loop(0, ROWS, unroll=4)
     def _(row):
         fraction = (half + jnp.minimum(row, ROWS - row)).astype(jnp.float32) / STRIDE
         product = dot(weight_own[...], mixed[row])
@@ -436,7 +451,7 @@
     def _():
         weight_halo[1] = weight_own[...]
 
-    @pl.loop(0, ROWS)
+    @pl.loop(0, ROWS, unroll=4)
     def _(row):
         fraction = (half - jnp.minimum(row, ROWS - row)).astype(jnp.float32) / STRIDE
         product = dot(weight_halo[row // half], mixed[row])
@@ -446,8 +461,16 @@
                 done[:, field * COLS:(field + 1) * COLS]
             )
 
+    copies = [
+        pltpu.make_async_copy(
+            result.at[pl.ds(field * MEMBERS, MEMBERS)],
+            out_hbm.at[pl.ds(field * MEMBERS, MEMBERS)],
+            out_sem.at[field],
+        )
+        for field in range(fields)
+    ]
     for field in range(fields):
-        @pl.loop(0, 8)
+        @pl.loop(0, 8, unroll=2)
         def _(chunk):
             first = pl.multiple_of(field * span + chunk * 256, 256)
             members = field * MEMBERS + chunk * 8
@@ -455,9 +478,10 @@
                 wide[pl.ds(first, 256), :].astype(jnp.bfloat16).reshape(8, ROWS, COLS)
             )
 
-    store = pltpu.make_async_copy(result, out_hbm, out_sem)
-    store.start()
-    store.wait()
+        copies[field].start()
+
+    for copy in copies:
+        copy.wait()
 
 
 def fused_body(state, obs_value, obs_sigma, obs_pixel, obs_route, obs_count, radius):
@@ -466,14 +490,20 @@
     arrivals = obs_value.shape[0]
     planes = fields * members
     anywhere = pl.BlockSpec(memory_space=pl.ANY)
-    local = pl.BlockSpec(memory_space=pltpu.VMEM)
     dma = pltpu.SemaphoreType.DMA
     analysis = pl.pallas_call(
         lambda *refs: kernel(peers, *refs),
         out_shape=jax.ShapeDtypeStruct((planes, tile_rows, tile_cols), jnp.bfloat16),
-        in_specs=[anywhere] + [local] * 5 + [pl.BlockSpec(memory_space=pltpu.SMEM)],
+        in_specs=[pl.BlockSpec(memory_space=pltpu.HBM)] * 7,
         out_specs=anywhere,
         scratch_shapes=[
+            pltpu.VMEM((1, arrivals), jnp.float32),
+            pltpu.VMEM((1, arrivals), jnp.float32),
+            pltpu.VMEM((1, arrivals), jnp.int32),
+            pltpu.VMEM((1, arrivals), jnp.int32),
+            pltpu.VMEM((1, 1), jnp.int32),
+            pltpu.VMEM(radius.shape[::-1], jnp.int32),
+            dma((6,)),
             pltpu.VMEM((planes, tile_rows, tile_cols), jnp.bfloat16),
             pltpu.VMEM((planes * tile_rows, tile_cols), jnp.float32),
             pltpu.VMEM((tile_rows, POINTS * members, fields * tile_cols), jnp.bfloat16),
@@ -487,10 +517,10 @@
             pltpu.VMEM((members, POINTS * members), jnp.bfloat16),
             pltpu.VMEM((2, members, POINTS * members), jnp.bfloat16),
             pltpu.VMEM((planes, tile_rows, tile_cols), jnp.bfloat16),
-            dma, dma, dma((peers,)), dma((peers,)), dma((2,)), dma((2,)), dma((2,)), dma((2,)),
+            dma, dma((fields,)), dma((peers,)), dma((peers,)), dma((2,)), dma((2,)), dma((2,)), dma((2,)),
         ],
         compiler_params=pltpu.CompilerParams(
-            collective_id=0, has_side_effects=True, vmem_limit_bytes=40 * 1024 * 1024
+            collective_id=0, has_side_effects=True, vmem_limit_bytes=63 * 1024 * 1024
         ),
     )(
         state.reshape(planes, tile_rows, tile_cols),
@@ -499,7 +529,7 @@
         obs_pixel.reshape(1, arrivals),
         obs_route.reshape(1, arrivals),
         obs_count.reshape(1, 1),
-        radius,
+        radius.T,
     )
     return analysis.reshape(state.shape)
 

time: 38.9 us -> 28.9 us (0.74)
  Pallas kernels: 32.1 us -> 25.2 us
  local copies, waits for them, and re-layouts: 5.93 us -> 2.86 us
    pallas_call x1, Pallas kernels: 32.1 us -> 25.2 us  [fused_body(): pl.pallas_call(lambda *refs: kernel(peers, *refs), out_shape=jax.ShapeDty...]
    unnamed x12 -> x1, local copies, waits for them, and re-layouts: 5.93 us -> 2.86 us
where the time goes in v2:
time: 28.9 us; the launch traced here: 28.7 us
  Pallas kernels  25.2 us (87%)
  local copies, waits for them, and re-layouts  2.86 us (10%)
  between operations  0.66 us (2%)
    pallas_call x1, Pallas kernels, fused_body(): pl.pallas_call(lambda *refs: kernel(peers, *refs), out_shape=jax.ShapeDty...  25.2 us
    unnamed x1, local copies, waits for them, and re-layouts  2.86 us

profile of v2, /device:TPU:1, one launch (start us, length us, event | category | flops | bytes accessed | tf_op | source)
XLA Modules:
  0.0 28.7 jit_solution(14086340900469671311)
XLA Ops:
  0.7 25.2 %shard_map.73 = bf16[192,32,128]{2,1,0:T(8,128)(2,1)} custom-call(bf16[192,32,128]{2,1,0:T(8,128)(2,1)} %bitcast.10, f32[1,64]{1,0:T(1,128)} %bitcast.12, f32[1,64]{1,0:T(1,128)} %bitcast.13, s32[1,64]{1,0:T(1,128)} %bitcast.14, s32[1,64]{1,0:T(1,128)} %bitcast.15, s32[1,1]{1,0:T(1,128)} %bitcast.8.refs_5_, s32[4,16]{1,0:T(4,128)} %bitcast.11), custom_call_target="tpu_custom_call" | custom-call | tf_op jit(solution)/shard_map/pallas_call | solution.py:494
  25.8 2.9 %copy.10 = bf16[3,64,32,128]{3,2,1,0:T(8,128)(2,1)} copy(bf16[3,64,32,128]{3,2,1,0:T(8,128)(2,1)} %bitcast.9) | data formatting | bytes 3145728

commit v3 on v2

--- a/solution.py
+++ b/solution.py
@@ -211,15 +211,20 @@
     factor = 1.5 * identity - 0.5 * current
     inverse_root = factor
     current = pair_matmul(current, factor, block_mask)
+    yield
     for iteration in range(1, ITER_NS):
         factor = 1.5 * identity - 0.5 * pair_matmul(inverse_root, current, block_mask)
+        yield
         if iteration < ITER_NS - 1:
             current = pair_matmul(current, factor, block_mask)
         inverse_root = pair_matmul(factor, inverse_root, block_mask)
+        yield
     square_root = inverse_root / jnp.sqrt(norm_scale)
     row = jnp.broadcast_to(forcing, (8, 2 * MEMBERS))
-    shift = pair_matmul(pair_matmul(row, square_root, block_mask), square_root, block_mask)
-    return (square_root + shift[0:1] / (MEMBERS - 1.0)).astype(jnp.bfloat16)
+    pulled = pair_matmul(row, square_root, block_mask)
+    yield
+    shift = pair_matmul(pulled, square_root, block_mask)
+    yield (square_root + shift[0:1] / (MEMBERS - 1.0)).astype(jnp.bfloat16)
 
 
 def kernel(
@@ -427,10 +432,14 @@
         more_gram, more_forcing = tile_gram(pack_halo[slot], offset)
         gram, forcing = gram + more_gram, forcing + more_forcing
     left = iota((1, 2 * MEMBERS), 1) < MEMBERS
+    solvers = []
     for pair in range(POINTS // 2):
         lanes = slice(pair * 2 * MEMBERS, (pair + 1) * 2 * MEMBERS)
         rows = jnp.where(left, forcing[2 * pair:2 * pair + 1], forcing[2 * pair + 1:2 * pair + 2])
-        weight_own[:, lanes] = solve_pair(gram[:, lanes], rows)
+        solvers.append(solve_pair(gram[:, lanes], rows))
+    for solved in zip(*solvers):
+        pass
+    weight_own[...] = jnp.concatenate(solved, axis=1)
     exchange(weight_own, weight_halo, weight_send, weight_recv)
 
     half = ROWS // 2

time: 28.9 us -> 27 us (0.934)
  Pallas kernels: 25.2 us -> 23.3 us
    pallas_call x1, Pallas kernels: 25.2 us -> 23.3 us  [fused_body(): pl.pallas_call(lambda *refs: kernel(peers, *refs), out_shape=jax.ShapeDty...]
where the time goes in v3:
time: 27 us; the launch traced here: 26.8 us
  Pallas kernels  23.3 us (86%)
  local copies, waits for them, and re-layouts  2.86 us (11%)
  between operations  0.66 us (2%)
    pallas_call x1, Pallas kernels, fused_body(): pl.pallas_call(lambda *refs: kernel(peers, *refs), out_shape=jax.ShapeDty...  23.3 us
    unnamed x1, local copies, waits for them, and re-layouts  2.86 us

profile of v3, /device:TPU:1, one launch (start us, length us, event | category | flops | bytes accessed | tf_op | source)
XLA Modules:
  0.0 26.8 jit_solution(1358125659287831867)
XLA Ops:
  0.7 23.3 %shard_map.73 = bf16[192,32,128]{2,1,0:T(8,128)(2,1)} custom-call(bf16[192,32,128]{2,1,0:T(8,128)(2,1)} %bitcast.10, f32[1,64]{1,0:T(1,128)} %bitcast.12, f32[1,64]{1,0:T(1,128)} %bitcast.13, s32[1,64]{1,0:T(1,128)} %bitcast.14, s32[1,64]{1,0:T(1,128)} %bitcast.15, s32[1,1]{1,0:T(1,128)} %bitcast.8.refs_5_, s32[4,16]{1,0:T(4,128)} %bitcast.11), custom_call_target="tpu_custom_call" | custom-call | tf_op jit(solution)/shard_map/pallas_call | solution.py:503
  24.0 2.9 %copy.10 = bf16[3,64,32,128]{3,2,1,0:T(8,128)(2,1)} copy(bf16[3,64,32,128]{3,2,1,0:T(8,128)(2,1)} %bitcast.9) | data formatting | bytes 3145728
